TPU v7x, 512 devices: a whole 4x4x16 slice. The times are simulated.
512 devices in a mesh: ctx: 64 (over z, x_lo, core), hg: 8 (over y, x_hi).
Axes of the slice: x: 4 (x_hi: 2, x_lo: 2; x = x_hi * 2 + x_lo), y: 4, z: 16, core: 2. Of those that a mesh axis runs over, the one named last changes fastest.
Arguments:
- hidden_in: bfloat16 [8192, 4096], P('ctx', 'hg')
- norm_gain: bfloat16 [4096], P('hg'), may hold values from 0.3984375 to 1.59375
- w_query: bfloat16 [4096, 4096], P('ctx', 'hg')
- w_key: bfloat16 [4096, 1024], P('ctx', 'hg')
- w_value: bfloat16 [4096, 1024], P('ctx', 'hg'), may hold values from -0.09375 to 0.09375
- block_mask: int32 [64, 64], replicated, may hold values from 0 to 1, as said below
Outputs:
- context: bfloat16 [8192, 4096], P('ctx', 'hg')
Inputs may be any that keep to these rules, and one draw needn't show every extreme that they name: `block_mask`: mask block b shows camera b % 8 at time b // 8; entry (i, j) is 1 only if j // 8 <= i // 8, and always where the two blocks show the same camera at such times, so the diagonal is 1.
All inputs are finite; a program needn't handle non-finite values.
Results may differ from a plain program's by a relative error of at most 0.0095.
Values may be sent and summed in bfloat16 or wider, within the bound.
A program may use at most 64 MiB of HBM per device.

v0:
```python
from functools import partial
import math

import jax
import jax.numpy as jnp
from jax import lax
from jax.sharding import PartitionSpec as P

HEAD_DIM = 128
BLOCK = 128


rope_base = 500000.0


def from_behind(block, axis, distance):
    devices = range(lax.axis_size(axis))
    route = [((i - distance) % len(devices), i) for i in devices]
    return lax.ppermute(block, axis, route)


def rotate(field, positions):
    half = field.shape[-1] // 2
    freq = rope_base ** (-jnp.arange(0, 2 * half, 2).astype(jnp.float32) / (2 * half))
    angles = positions[:, None] * freq[None, :]
    cosine = jnp.cos(angles)[:, None, :]
    sine = jnp.sin(angles)[:, None, :]
    first = field[..., :half]
    second = field[..., half:]
    return jnp.concatenate(
        [first * cosine - second * sine, second * cosine + first * sine], axis=-1
    )


def shards(hidden_in, norm_gain, w_query, w_key, w_value, block_mask):
    whole, gain_all = (
        lax.all_gather(hidden_in, "hg", axis=1, tiled=True),
        lax.all_gather(norm_gain, "hg", axis=0, tiled=True),
    )
    values = whole.astype(jnp.float32)
    inverse = lax.rsqrt(jnp.mean(values * values, axis=-1, keepdims=True) + 1e-05)
    normed = (values * inverse * gain_all.astype(jnp.float32)).astype(jnp.bfloat16)
    rows = normed.shape[0]

    def add_rows(piece):
        return jnp.dot(normed, piece, preferred_element_type=jnp.float32)

    query = add_rows(lax.all_gather(w_query, "ctx", axis=0, tiled=True))
    key = add_rows(lax.all_gather(w_key, "ctx", axis=0, tiled=True))
    value = add_rows(lax.all_gather(w_value, "ctx", axis=0, tiled=True))
    head_dim = HEAD_DIM
    kv_local = w_key.shape[1] // head_dim
    q_local = w_query.shape[1] // head_dim
    group = q_local // kv_local
    me = lax.axis_index("ctx")
    count = lax.axis_size("ctx")
    positions = (me * rows + jnp.arange(rows)).astype(jnp.float32)
    query_rot = rotate(query.reshape(rows, q_local, head_dim), positions).astype(jnp.bfloat16)
    query_rot = query_rot.reshape(rows, kv_local, group, head_dim)
    key_rot = rotate(key.reshape(rows, kv_local, head_dim), positions).astype(jnp.bfloat16)
    value_heads = value.astype(jnp.bfloat16).reshape(rows, kv_local, head_dim)
    per_dev = rows // BLOCK
    mask_rows = lax.dynamic_slice_in_dim(block_mask, me * per_dev, per_dev, 0)
    scale = head_dim ** (-0.5)

    def compute(mask_tile, keys, vals, carry):
        running, total, summed = carry
        allowed = jnp.repeat(jnp.repeat(mask_tile > 0, BLOCK, axis=0), BLOCK, axis=1)[None, None]
        scores = (
            jnp.einsum("qhgd,khd->hgqk", query_rot, keys, preferred_element_type=jnp.float32)
            * scale
        )
        masked = jnp.where(allowed, scores, jnp.float32(-1e30))
        newmax = jnp.maximum(running, jnp.max(masked, axis=-1))
        weights = jnp.where(allowed, jnp.exp(masked - newmax[..., None]), jnp.float32(0.0))
        factor = jnp.exp(running - newmax)
        total = total * factor + jnp.sum(weights, axis=-1)
        summed = summed * factor[..., None] + jnp.einsum(
            "hgqk,khd->hgqd", weights.astype(jnp.bfloat16), vals, preferred_element_type=jnp.float32
        )
        return (newmax, total, summed)

    def update(state, keys, vals, key_start):
        key_count = keys.shape[0]
        span_keys = math.gcd(key_count, 1024)
        offset = 0 * span_keys
        mask_tile = lax.dynamic_slice_in_dim(
            mask_rows, (key_start + offset) // BLOCK, span_keys // BLOCK, 1
        )
        return lax.cond(
            jnp.any(mask_tile > 0),
            partial(compute, mask_tile, keys, vals),
            lambda inner: inner,
            state,
        )

    empty_state = (
        jnp.full((kv_local, group, rows), -1e30, jnp.float32),
        jnp.zeros((kv_local, group, rows), jnp.float32),
        jnp.zeros((kv_local, group, rows, head_dim), jnp.float32),
    )
    state = update(empty_state, key_rot, value_heads, me * rows)

    def turn(step, carry):
        current, keys, vals = carry
        keys, vals = from_behind((keys, vals), "ctx", 1)
        return (update(current, keys, vals, (me - step) % count * rows), keys, vals)

    state = lax.fori_loop(1, count, turn, (state, key_rot, value_heads))[0]
    running, total, summed = state
    result = summed / total[..., None]
    return (
        jnp.transpose(result, (2, 0, 1, 3)).reshape(rows, q_local * head_dim).astype(jnp.bfloat16)
    )


def solution(mesh):
    placed = (P("ctx", "hg"), P("hg"), P("ctx", "hg"), P("ctx", "hg"), P("ctx", "hg"), P())
    return jax.shard_map(
        shards, mesh=mesh, in_specs=placed, out_specs=P("ctx", "hg"), check_vma=False
    )
```

profile of v0, /device:TPU:384, one launch (start us, length us, event | category | flops | bytes accessed | tf_op | source)
XLA Modules:
  0.0 1064.9 jit_solution(17691903131944226651)
XLA Ops:
  10.0 31.0 %all-gather = bf16[8,1,512]{2,1,0:T(2,128)(2,1)S(1)} all-gather(bf16[1,1,512]{2,1,0:T(2,128)(2,1)S(1)} %reshape.313), channel_id=1, replica_groups=mesh['ctx'=64,'hg'=8] {'hg'}, dimensions={0}, use_global_device_ids=true | all-gather | bytes 9216 | tf_op jit(solution)/shard_map/all_gather | solution.py:38
  44.0 27.2 %all-gather.6.cloned.1.call-done = bf16[128,4096]{1,0:T(8,128)(2,1)} async-done(((bf16[128,512]{1,0:T(8,128)(2,1)}), bf16[128,4096]{1,0:T(8,128)(2,1)}) %all-gather.6.cloned.1.call-update) | async-done | bytes 1048592 | tf_op jit(solution)/shard_map/all_gather | solution.py:37
  72.8 116.9 %all-gather.8.cloned.1.call-done = bf16[4096,128]{1,0:T(8,128)(2,1)} async-done(((bf16[64,128]{1,0:T(8,128)(2,1)}), bf16[4096,128]{1,0:T(8,128)(2,1)}) %all-gather.8.cloned.1.call-update) | async-done | bytes 1048592 | tf_op jit(solution)/shard_map/all_gather | solution.py:49
  189.8 2.2 convolution_bitcast_fusion.1
  192.3 116.7 %all-gather.12.cloned.1.call-done = bf16[4096,128]{1,0:T(8,128)(2,1)} async-done(((bf16[64,128]{1,0:T(8,128)(2,1)}), bf16[4096,128]{1,0:T(8,128)(2,1)}) %all-gather.12.cloned.1.call-update) | async-done | bytes 1048592 | tf_op jit(solution)/shard_map/all_gather | solution.py:50
  310.7 121.0 %all-gather.10.cloned.1.call-done = bf16[4096,512]{1,0:T(8,128)(2,1)} async-done(((bf16[64,512]{1,0:T(8,128)(2,1)}), bf16[4096,512]{1,0:T(8,128)(2,1)}) %all-gather.10.cloned.1.call-update) | async-done | bytes 4194320 | tf_op jit(solution)/shard_map/all_gather | solution.py:48
  431.7 3.0 fusion.46
  436.4 621.0 %while.23 = (s32[]{:T(128)}, f32[1,4,128]{2,1,0:T(4,128)S(1)}, f32[1,4,128]{2,1,0:T(4,128)S(1)}, f32[1,4,128,128]{3,2,1,0:T(8,128)S(1)}, bf16[128,1,128]{2,0,1:T...) while((s32[]{:T(128)}, f32[1,4,128]{2,1,0:T(4,128)S(1)}, ...), condition=%wide.region_10.11_spmd, body=%wide.region_5.10_spmd.sunk | while | flops 34276896 | bytes 1934008 | solution.py:109
  436.5 2.1 collective-permute-start
  443.8 2.1 collective-permute-done.1
  452.5 2.1 collective-permute-done
  461.8 2.1 collective-permute-done
  471.1 2.1 collective-permute-done
  481.6 2.1 collective-permute-done
  492.2 2.1 collective-permute-done
  501.5 2.1 collective-permute-done
  522.6 2.1 collective-permute-done
  531.9 2.1 collective-permute-done
  542.4 2.1 collective-permute-done
  551.7 2.1 collective-permute-done
  659.0 2.1 collective-permute-done
  668.3 2.1 collective-permute-done
  698.7 2.1 collective-permute-done
  708.0 2.1 collective-permute-done
  737.1 2.1 collective-permute-done
  747.7 2.1 collective-permute-done
  758.2 2.1 collective-permute-done
  768.8 2.1 collective-permute-done
  779.3 2.1 collective-permute-done
  788.6 2.1 collective-permute-done
  799.2 2.1 collective-permute-done
  808.5 2.1 collective-permute-done
  819.0 2.1 collective-permute-done
  828.3 2.1 collective-permute-done
  878.6 2.1 collective-permute-done
  887.9 2.1 collective-permute-done
  897.2 2.1 collective-permute-done
  907.7 2.1 collective-permute-done
  918.3 2.1 collective-permute-done
  927.6 2.1 collective-permute-done
  936.9 2.1 collective-permute-done
  946.2 2.1 collective-permute-done
  955.5 2.1 collective-permute-done
  964.8 2.1 collective-permute-done
  974.1 2.1 collective-permute-done
  1012.5 2.1 collective-permute-done
  1021.8 2.1 collective-permute-done
  1032.3 2.1 collective-permute-done
  (668 shorter events, 516.6 us)
Async XLA Ops:
  6.5 64.7 %all-gather.6.cloned.1.call-start = ((), (), s32[]{:S(2)}) async-start(), calls=%async_computation | async-start | bytes 1179648 | tf_op jit(solution)/shard_map/all_gather | solution.py:37
  7.3 182.5 %all-gather.8.cloned.1.call-start = ((), (), s32[]{:S(2)}) async-start(), calls=%async_computation.1 | async-start | bytes 1064960 | tf_op jit(solution)/shard_map/all_gather | solution.py:49
  8.0 300.9 %all-gather.12.cloned.1.call-start = ((), (), s32[]{:S(2)}) async-start(), calls=%async_computation.3 | async-start | bytes 1064960 | tf_op jit(solution)/shard_map/all_gather | solution.py:50
  8.7 423.0 %all-gather.10.cloned.1.call-start = ((), (), s32[]{:S(2)}) async-start(), calls=%async_computation.2 | async-start | bytes 4259840 | tf_op jit(solution)/shard_map/all_gather | solution.py:48
  436.5 7.3 collective-permute-start
  438.6 7.3 collective-permute-start.1
  447.2 7.3 collective-permute-start
  449.2 7.3 collective-permute-start.1
  456.5 7.3 collective-permute-start
  458.4 7.3 collective-permute-start.1
  465.8 7.3 collective-permute-start
  467.7 7.3 collective-permute-start.1
  476.4 7.3 collective-permute-start
  478.3 7.3 collective-permute-start.1
  486.9 7.3 collective-permute-start
  488.8 7.3 collective-permute-start.1
  496.2 7.3 collective-permute-start
  498.1 7.3 collective-permute-start.1
  506.8 7.3 collective-permute-start
  508.7 7.3 collective-permute-start.1
  517.3 7.3 collective-permute-start
  519.2 7.3 collective-permute-start.1
  526.6 7.3 collective-permute-start
  528.5 7.3 collective-permute-start.1
  537.2 7.3 collective-permute-start
  539.1 7.3 collective-permute-start.1
  546.5 7.3 collective-permute-start
  548.4 7.3 collective-permute-start.1
  557.0 7.3 collective-permute-start
  558.9 7.3 collective-permute-start.1
  566.3 7.3 collective-permute-start
  586.8 7.3 collective-permute-start.1
  595.5 7.3 collective-permute-start
  597.4 7.3 collective-permute-start.1
  606.0 7.3 collective-permute-start
  607.9 7.3 collective-permute-start.1
  615.3 7.3 collective-permute-start
  617.2 7.3 collective-permute-start.1
  625.8 7.3 collective-permute-start
  646.4 7.3 collective-permute-start.1
  653.7 7.3 collective-permute-start
  655.7 7.3 collective-permute-start.1
  663.0 7.3 collective-permute-start
  665.0 7.3 collective-permute-start.1
  673.6 7.3 collective-permute-start
  675.5 7.3 collective-permute-start.1
  682.9 7.3 collective-permute-start
  684.8 7.3 collective-permute-start.1
  (83 other events, 839.9 us)
Sparse Core Ops, SparseCore 0:
  10.4 60.7 all-gather.5
  73.4 116.3 all-gather.7
  191.9 116.9 all-gather.11
  310.9 120.7 all-gather.9
where the time goes:
time: 1070 us; the launch traced here: 1060 us
  waiting for transfers between devices  637 us (60%)
  starting transfers between devices  242 us (23%)
  loops' own time  68.7 us (6%)
  other arithmetic  47 us (4%)
  blocking collectives  31 us (3%)
  matrix products  20.5 us (2%)
  between operations  13.9 us (1%)
    ppermute x126, waiting for transfers between devices, from_behind(): return lax.ppermute(block, axis, route)  253 us
    ppermute x126, starting transfers between devices, from_behind(): return lax.ppermute(block, axis, route)  242 us
    all_gather x1, waiting for transfers between devices, shards(): query = add_rows(lax.all_gather(w_query, 'ctx', axis=0, tiled=True))  121 us
    all_gather x1, waiting for transfers between devices, shards(): key = add_rows(lax.all_gather(w_key, 'ctx', axis=0, tiled=True))  117 us
    all_gather x1, waiting for transfers between devices, shards(): value = add_rows(lax.all_gather(w_value, 'ctx', axis=0, tiled=True))  117 us
    another operation x1, loops' own time, shards(): state = lax.fori_loop(1, count, turn, (state, key_rot, value_heads))[0]  49.3 us
    gt x63, other arithmetic, update(): mask_tile > 0  42 us
    all_gather x1, blocking collectives, shards(): lax.all_gather(norm_gain, 'hg', axis=0, tiled=True)  31 us
  transfers between devices with their start and end apart: 130, of which 130 were waited for; matrix products, arithmetic and copies ran while one was open for 5% of the time, Pallas kernels for 0%

commit v1 on v0

v1 whole, which is shorter than its diff:
```python
import math

import jax
import jax.numpy as jnp
from jax import lax
from jax.experimental import pallas as pl
from jax.experimental.pallas import tpu as pltpu
from jax.sharding import PartitionSpec as P

MESH = pl.DeviceIdType.MESH
BF16, F32 = jnp.bfloat16, jnp.float32
NZ, NY = 16, 4
ROWS = 128
ROPE_BASE = 500000.0
EXP_SCALE = 128 ** (-0.5) * math.log2(math.e)
BIG = 1e30
UP, DOWN = 8, 7

Z_UP, Z_DN = 0, 8
C_OWN, C_UP, C_DN = 15, 16, 24
PLAIN = 31
X_OWN, X_UP, X_DN = 31, 32, 40
CX_OWN, CX_UP, CX_DN = 47, 48, 56
FULL = 63


def kernel(
    x_ref, gain_ref, wq_ref, wk_ref, wv_ref, cos_ref, sin_ref, mask_ref, o_ref,
    xs, xbuf, nb, wkv, wq, kv, sq, pkv, pq, qt, m_ref, l_ref, acc,
    x_s, x_r, wkv_s, wkv_r, wq_s, wq_r, kv_s, kv_r, p_s, p_r,
):
    c = lax.axis_index("ctx")
    g = lax.axis_index("hg")
    z, xl, co = c // 4, (c // 2) % 2, c % 2
    y, xh = g // 2, g % 2

    def device(dz=0, flip_x=False, flip_c=False, dy=0, flip_h=False):
        zz = (z + dz + NZ) % NZ
        yy = (y + dy + NY) % NY
        a = 1 - xl if flip_x else xl
        b = 1 - co if flip_c else co
        h = 1 - xh if flip_h else xh
        return (zz * 4 + a * 2 + b, yy * 2 + h)

    up1, dn1, up2, dn2 = device(dz=1), device(dz=-1), device(dz=2), device(dz=-2)
    core, xp = device(flip_c=True), device(flip_x=True)
    hp, xx = device(flip_h=True), device(flip_x=True, flip_h=True)
    yu, yd = device(dy=1), device(dy=-1)
    peers = (up1, dn1, up2, dn2, core, xp, hp, xx, yu, yd)

    bar = pltpu.get_barrier_semaphore()
    for p in peers:
        pl.semaphore_signal(bar, inc=1, device_id=p, device_id_type=MESH)

    gain = jnp.broadcast_to(gain_ref[...].astype(F32), (16, 512)).astype(BF16)
    for q in range(2):
        for k in range(2):
            lanes = pl.ds((2 * k + q) * 128, 128)
            xs[q, pl.ds(0, ROWS), pl.ds(k * 128, 128)] = x_ref[:, lanes]
            xs[q, pl.ds(ROWS, 16), pl.ds(k * 128, 128)] = gain[:, (2 * k + q) * 128 : (2 * k + q + 1) * 128]
    xbuf[g, xl] = xs[xl]
    wkv[z, co, :, pl.ds(0, 128)] = wk_ref[...]
    wkv[z, co, :, pl.ds(128, 128)] = wv_ref[...]
    wq[z, co] = wq_ref[...]

    pl.semaphore_wait(bar, len(peers))

    started = []

    def send(src, dst, ssem, rsem, dev):
        copy = pltpu.make_async_remote_copy(
            src_ref=src, dst_ref=dst, send_sem=ssem, recv_sem=rsem,
            device_id=dev, device_id_type=MESH,
        )
        copy.start()
        started.append(copy)

    def arrive(dst, ssem, rsem):
        pltpu.make_async_remote_copy(
            src_ref=dst, dst_ref=dst, send_sem=ssem, recv_sem=rsem,
            device_id=core, device_id_type=MESH,
        ).wait_recv()

    class Stream:
        def __init__(self, slot, ssem, rsem, across):
            self.slot, self.s, self.r, self.across = slot, ssem, rsem, across

        def push(self, at, place, dev):
            ref = self.slot(*at)
            send(ref, ref, self.s.at[place], self.r.at[place], dev)

        def take(self, at, place):
            arrive(self.slot(*at), self.s.at[place], self.r.at[place])

        def own(self):
            at = (z, xl, co)
            self.push(at, Z_UP + 1, up2)
            self.push(at, Z_DN + 1, dn2)
            self.push(at, Z_UP, up1)
            self.push(at, Z_DN, dn1)
            if self.across:
                self.push(at, X_OWN, xp)
            self.push(at, C_OWN, core)

        def up(self, d):
            at = ((z - d + NZ) % NZ, xl, co)
            self.take(at, Z_UP + d - 1)
            if d % 2 == 0 and d < UP:
                self.push(at, Z_UP + d + 1, up2)
                self.push(at, Z_UP + d, up1)
            if self.across:
                self.push(at, X_UP + d - 1, xp)
            self.push(at, C_UP + d - 1, core)

        def down(self, d):
            at = ((z + d) % NZ, xl, co)
            self.take(at, Z_DN + d - 1)
            if d % 2 == 0 and d < DOWN:
                if d + 2 <= DOWN:
                    self.push(at, Z_DN + d + 1, dn2)
                self.push(at, Z_DN + d, dn1)
            if self.across:
                self.push(at, X_DN + d - 1, xp)
            self.push(at, C_DN + d - 1, core)

        def step(self, k):
            for d in (2 * k, 2 * k - 1):
                self.up(d)
                if d <= DOWN:
                    self.down(d)

        def from_core(self):
            oc = 1 - co
            self.take((z, xl, oc), C_OWN)
            for d in range(1, UP + 1):
                self.take(((z - d + NZ) % NZ, xl, oc), C_UP + d - 1)
            for d in range(1, DOWN + 1):
                self.take(((z + d) % NZ, xl, oc), C_DN + d - 1)

    kvw = Stream(lambda zz, a, b: wkv.at[zz, b], wkv_s, wkv_r, False)
    qw = Stream(lambda zz, a, b: wq.at[zz, b], wq_s, wq_r, False)
    both = Stream(lambda zz, a, b: kv.at[zz * 4 + a * 2 + b], kv_s, kv_r, True)

    pieces = ((xh, xl), (xh, 1 - xl), (1 - xh, xl), (1 - xh, 1 - xl))

    def x_push(src, i, yy, place, dev):
        h, t = pieces[i]
        send(src, xbuf.at[yy * 2 + h, t], x_s.at[place], x_r.at[place], dev)

    def x_take(i, yy, place):
        h, t = pieces[i]
        arrive(xbuf.at[yy * 2 + h, t], x_s.at[place], x_r.at[place])

    def x_held(i, yy):
        h, t = pieces[i]
        return xbuf.at[yy * 2 + h, t]

    kvw.own()
    for i, dev, part in ((1, xp, 1 - xl), (2, hp, xl), (3, xx, 1 - xl)):
        send(xs.at[part], xbuf.at[g, xl], x_s.at[i - 1], x_r.at[i - 1], dev)
    for i in range(4):
        if i > 0:
            x_take(i, y, i - 1)
        x_push(x_held(i, y), i, y, 3 + i, yu)
        x_push(x_held(i, y), i, y, 7 + i, yd)
        if i == 0:
            qw.own()
    below, above, far = (y + NY - 1) % NY, (y + 1) % NY, (y + 2) % NY

    def x_turn(i):
        x_take(i, below, 3 + i)
        if i < 2:
            x_push(x_held(i, below), i, below, 11 + i, yu)
        x_take(i, above, 7 + i)
        if i >= 2:
            x_push(x_held(i, above), i, above, 11 + i, yd)

    kvw.step(1)
    x_turn(0)
    x_turn(1)
    qw.step(1)
    kvw.step(2)
    x_turn(2)
    x_turn(3)
    qw.step(2)
    for i in range(4):
        x_take(i, far, 11 + i)

    eye = lax.broadcasted_iota(jnp.int32, (ROWS, ROWS), 0) == lax.broadcasted_iota(jnp.int32, (ROWS, ROWS), 1)
    sq[0] = jnp.zeros((8, 128), F32)
    for t in range(2):
        col = jnp.zeros((ROWS, 256), F32)
        for h in range(8):
            v = xbuf[h, t, pl.ds(0, ROWS)].astype(F32)
            col += v * v
        col = jnp.sum(col, axis=1, keepdims=True)
        sq[0, pl.ds(t, 1)] = jnp.sum(jnp.where(eye, col, 0.0), axis=0, keepdims=True)
    send(sq.at[0], sq.at[1], p_s.at[0], p_r.at[0], xp)
    kvw.step(3)
    qw.step(3)
    arrive(sq.at[1], p_s.at[0], p_r.at[0])
    for t in range(2):
        total = sq[0, pl.ds(t, 1)] + sq[1, pl.ds(t, 1)]
        inv = lax.rsqrt(total * (1.0 / 4096) + 1e-05)
        inv = jnp.sum(jnp.where(eye, inv, 0.0), axis=1, keepdims=True)
        for h in range(8):
            v = xbuf[h, t, pl.ds(0, ROWS)].astype(F32)
            scale = xbuf[h, t, pl.ds(ROWS, 16)].astype(F32)[0:1]
            nb[h, pl.ds(t * ROWS, ROWS)] = (v * inv * scale).astype(BF16)
    kvw.step(4)
    kvw.from_core()

    def project(w, cols, first):
        rows = pl.ds(first * ROWS, ROWS)
        out = jnp.zeros((ROWS, cols), F32)
        for h in range(8):
            out += jnp.dot(
                nb[h, rows], w[pl.ds(2 * h, 2)].reshape(256, cols), preferred_element_type=F32
            )
        return out

    cos, sin = cos_ref[...], sin_ref[...]

    def rotate(v):
        swapped = jnp.concatenate([v[:, 64:], v[:, :64]], axis=1)
        return v * cos + swapped * sin

    pkv[0] = project(wkv, 256, 1 - xl)
    send(pkv.at[0], pkv.at[1], p_s.at[1], p_r.at[1], xp)
    mine = project(wkv, 256, xl)
    arrive(pkv.at[1], p_s.at[1], p_r.at[1])
    mine = mine + pkv[1]
    kv[c, :, pl.ds(0, 128)] = rotate(mine[:, :128]).astype(BF16)
    kv[c, :, pl.ds(128, 128)] = mine[:, 128:].T.astype(BF16)
    both.own()
    qw.step(4)
    both.step(1)
    qw.from_core()
    pq[0] = project(wq, 512, 1 - xl)
    send(pq.at[0], pq.at[1], p_s.at[2], p_r.at[2], xp)
    pq[2] = project(wq, 512, xl)
    both.step(2)
    arrive(pq.at[1], p_s.at[2], p_r.at[2])
    for h in range(4):
        lanes = pl.ds(h * 128, 128)
        qt[:, lanes] = rotate(pq[1, :, lanes] + pq[2, :, lanes]).T.astype(BF16)

    m_ref[...] = jnp.full((1, 512), -BIG, F32)
    l_ref[...] = jnp.zeros((1, 512), F32)
    acc[...] = jnp.zeros((128, 512), F32)

    def attend(zz):
        held = kv[pl.ds(zz * 4, 4)]
        keys = held[:, :, :128].reshape(512, 128)
        vals = jnp.concatenate([held[j, :, 128:] for j in range(4)], axis=1)
        scores = jnp.dot(keys, qt[...], preferred_element_type=F32)
        old = m_ref[...]
        new = old
        shut = []
        for j in range(4):
            shut.append((1 - mask_ref[c, zz * 4 + j]).astype(F32) * BIG)
            top = jnp.max(scores[j * 128 : (j + 1) * 128], axis=0, keepdims=True)
            new = jnp.maximum(new, top * EXP_SCALE - shut[j])
        factor = jnp.exp2(old - new)
        total = l_ref[...] * factor
        parts = []
        for j in range(4):
            w = jnp.exp2(scores[j * 128 : (j + 1) * 128] * EXP_SCALE - (new + shut[j]))
            total = total + jnp.sum(w, axis=0, keepdims=True)
            parts.append(w.astype(BF16))
        m_ref[...] = new
        l_ref[...] = total
        acc[...] = acc[...] * factor + jnp.dot(
            vals, jnp.concatenate(parts, axis=0), preferred_element_type=F32
        )

    oc, ox = 1 - co, 1 - xl

    def cross(at, x_place, cx_place):
        both.take((at, ox, co), x_place)
        both.push((at, ox, co), cx_place, core)

    def gather_rest(at, c_place, cx_place):
        both.take((at, xl, oc), c_place)
        both.take((at, ox, oc), cx_place)

    cross(z, X_OWN, CX_OWN)
    gather_rest(z, C_OWN, CX_OWN)
    attend(z)
    both.step(3)
    ups = lambda d: (z - d + NZ) % NZ
    dns = lambda d: (z + d) % NZ

    def crosses(k):
        for d in (2 * k, 2 * k - 1):
            cross(ups(d), X_UP + d - 1, CX_UP + d - 1)
            if d <= DOWN:
                cross(dns(d), X_DN + d - 1, CX_DN + d - 1)

    def attends(k):
        for d in (2 * k, 2 * k - 1):
            gather_rest(ups(d), C_UP + d - 1, CX_UP + d - 1)
            attend(ups(d))
            if d <= DOWN:
                gather_rest(dns(d), C_DN + d - 1, CX_DN + d - 1)
                attend(dns(d))

    crosses(1)
    attends(1)
    both.step(4)
    for k in (2, 3, 4):
        crosses(k)
        attends(k)

    inverse = 1.0 / l_ref[...]
    for h in range(4):
        lanes = pl.ds(h * 128, 128)
        o_ref[:, lanes] = (acc[:, lanes] * inverse[:, h * 128 : (h + 1) * 128]).T.astype(BF16)
    for copy in started:
        copy.wait_send()


def shards(hidden_in, norm_gain, w_query, w_key, w_value, block_mask):
    positions = (lax.axis_index("ctx") * ROWS + jnp.arange(ROWS)).astype(F32)
    freq = ROPE_BASE ** (-jnp.arange(0, 128, 2).astype(F32) / 128)
    angles = positions[:, None] * freq[None, :]
    cosine, sine = jnp.cos(angles), jnp.sin(angles)
    cos = jnp.concatenate([cosine, cosine], axis=1)
    sin = jnp.concatenate([-sine, sine], axis=1)
    vmem = pl.BlockSpec(memory_space=pltpu.VMEM)
    dma = pltpu.SemaphoreType.DMA
    return pl.pallas_call(
        kernel,
        out_shape=jax.ShapeDtypeStruct((ROWS, 512), BF16),
        in_specs=[vmem] * 7 + [pl.BlockSpec(memory_space=pltpu.SMEM)],
        out_specs=vmem,
        scratch_shapes=[
            pltpu.VMEM((2, ROWS + 16, 256), BF16),
            pltpu.VMEM((8, 2, ROWS + 16, 256), BF16),
            pltpu.VMEM((8, 2 * ROWS, 256), BF16),
            pltpu.VMEM((NZ, 2, 64, 256), BF16),
            pltpu.VMEM((NZ, 2, 64, 512), BF16),
            pltpu.VMEM((64, ROWS, 256), BF16),
            pltpu.VMEM((2, 8, 128), F32),
            pltpu.VMEM((2, ROWS, 256), F32),
            pltpu.VMEM((3, ROWS, 512), F32),
            pltpu.VMEM((128, 512), BF16),
            pltpu.VMEM((1, 512), F32),
            pltpu.VMEM((1, 512), F32),
            pltpu.VMEM((128, 512), F32),
            dma((15,)), dma((15,)),
            dma((PLAIN,)), dma((PLAIN,)),
            dma((PLAIN,)), dma((PLAIN,)),
            dma((FULL,)), dma((FULL,)),
            dma((3,)), dma((3,)),
        ],
        compiler_params=pltpu.CompilerParams(
            collective_id=0, has_side_effects=True, vmem_limit_bytes=48 * 2**20
        ),
        cost_estimate=pl.CostEstimate(flops=3 * 10**9, bytes_accessed=2**20, transcendentals=4 * 2**20),
    )(hidden_in, norm_gain.reshape(1, 512), w_query, w_key, w_value, cos, sin, block_mask)


def solution(mesh):
    placed = (P("ctx", "hg"), P("hg"), P("ctx", "hg"), P("ctx", "hg"), P("ctx", "hg"), P())
    return jax.shard_map(
        shards, mesh=mesh, in_specs=placed, out_specs=P("ctx", "hg"), check_vma=False
    )
```

time: 1070 us -> 87.4 us (0.08)
  the two profiles are of different devices: /device:TPU:384 before, /device:TPU:1 now
where the time goes in v1:
time: 87.4 us; the launch traced here: 87.3 us
  Pallas kernels  85.3 us (98%)
  local copies, waits for them, and re-layouts  1.42 us (2%)
    pallas_call x1, Pallas kernels, shards(): pl.pallas_call(kernel, out_shape=jax.ShapeDtypeStruct((ROWS, 512), BF16),...  85.3 us

profile of v1, /device:TPU:1, one launch (start us, length us, event | category | flops | bytes accessed | tf_op | source)
XLA Modules:
  0.0 87.3 jit_solution(7182552309256020809)
XLA Ops:
  0.0 0.3 fusion
  0.3 0.0 copy-start
  0.3 0.0 copy-start.1
  0.4 0.0 copy-start.2
  0.4 0.0 copy-start.3
  0.4 0.0 copy-start.4
  0.4 0.1 pad_maximum_fusion
  0.5 0.0 copy-start.5
  0.5 0.7 copy-done.5
  1.2 0.1 copy-done
  1.2 0.0 copy-done.1
  1.2 0.0 copy-done.2
  1.2 0.0 copy-done.3
  1.2 0.0 copy-done.4
  1.3 85.3 %shard_map.64 = bf16[128,512]{1,0:T(8,128)(2,1)S(1)} custom-call(bf16[128,512]{1,0:T(8,128)(2,1)S(1)} %copy-done, bf16[1,512]{1,0:T(2,128)(2,1)S(1)} %reshape.16.gain_ref, bf16[64,512]{1,0:T(8,128)(2,1)S(1)} %copy-done.1, bf16[64,128]{1,0:T(8,128)(2,1)S(1)} %copy-done.3, bf16[64,128]{1,0:T(8,128)(2,1)S(1)} %copy-done.4, ...), custom_call_target="tpu_custom_call" | custom-call | flops 3000000000 | bytes 1048576 | tf_op jit(solution)/shard_map/pallas_call | solution.py:332
  86.6 0.7 copy.8
  (3 shorter events, 0.0 us)
Async XLA Ops:
  0.3 0.9 %copy-start = (bf16[128,512]{1,0:T(8,128)(2,1)S(1)}, bf16[128,512]{1,0:T(8,128)(2,1)}, u32[]{:S(2)}) copy-start(bf16[128,512]{1,0:T(8,128)(2,1)} %x_ref.1) | copy-start | bytes 393220
  0.3 0.9 %copy-start.1 = (bf16[64,512]{1,0:T(8,128)(2,1)S(1)}, bf16[64,512]{1,0:T(8,128)(2,1)}, u32[]{:S(2)}) copy-start(bf16[64,512]{1,0:T(8,128)(2,1)} %wq_ref.1) | copy-start | bytes 196612
  0.4 0.9 %copy-start.2 = (s32[64,64]{1,0:T(8,128)S(1)}, s32[64,64]{1,0:T(8,128)}, u32[]{:S(2)}) copy-start(s32[64,64]{1,0:T(8,128)} %mask_ref.1) | copy-start | bytes 49156
  0.4 0.9 %copy-start.3 = (bf16[64,128]{1,0:T(8,128)(2,1)S(1)}, bf16[64,128]{1,0:T(8,128)(2,1)}, u32[]{:S(2)}) copy-start(bf16[64,128]{1,0:T(8,128)(2,1)} %wk_ref.1) | copy-start | bytes 49156
  0.4 0.9 copy-start.4
  0.5 0.7 copy-start.5
